TPU v7x, 32 devices: a whole 2x2x4 slice. The times are simulated.
32 devices in a mesh: gx: 4 (over y, core), gy: 8 (over z, x).
Axes of the slice: x: 2, y: 2, z: 4, core: 2. Of those that a mesh axis runs over, the one named last changes fastest.
Arguments:
- start_vector: float32 [2, 16, 64, 1024], P(None, None, 'gx', 'gy'), may hold values from -6 to 6
- viscosity: float32 [16, 64, 1024], P(None, 'gx', 'gy'), may hold values from 0.1 to 10
- friction: float32 [16, 64, 1024], P(None, 'gx', 'gy'), may hold values from 0.5 to 5
- shifts: float32 [8], replicated, may hold values from 0.2 to 1.6, as said below
Outputs:
- orthonormal: float32 [9, 2, 16, 64, 1024], P(None, None, None, 'gx', 'gy')
- factor: float32 [9, 9], replicated
Inputs may be any that keep to these rules, and one draw needn't show every extreme that they name: The 8 shifts are distinct, one in each of 8 equal parts of the range.
All inputs are finite; a program needn't handle non-finite values.
Results may differ from a plain program's by a relative error of at most 0.00035.
Values sent between devices are 32-bit elements; how exact they have to be, the bound alone decides.
A program may use at most 128 MiB of HBM per device.

v0:
```python
import jax
import jax.numpy as jnp
from jax import lax
from jax.sharding import PartitionSpec as P

cross_gain = 1.0


def extended(shard, sides, width):
    for axis, dim in sides:
        peers, length = (lax.axis_size(axis), shard.shape[dim])
        up = [(i, (i + 1) % peers) for i in range(peers - 1)]
        down = [(j, i) for i, j in up]
        last = lax.slice_in_dim(shard, length - width, length, axis=dim)
        first = lax.slice_in_dim(shard, 0, width, axis=dim)
        before = lax.ppermute(last, axis, up)
        after = lax.ppermute(first, axis, down)
        shard = jnp.concatenate([before, shard, after], axis=dim)
    return shard


def neighbour_offsets():
    offsets = []
    for shift_z in (-1, 0, 1):
        for shift_x in (-1, 0, 1):
            for shift_y in (-1, 0, 1):
                distance = abs(shift_z) + abs(shift_x) + abs(shift_y)
                if distance == 0:
                    continue
                offsets.append((shift_z, shift_x, shift_y, 0.5 ** (distance - 1)))
    return offsets


def apply_operator(field_pad, eta_pad, friction, region_mask):
    levels = friction.shape[0]
    row_count = field_pad.shape[2] - 2
    col_count = field_pad.shape[3] - 2
    eta_z = jnp.pad(eta_pad, ((1, 1), (0, 0), (0, 0)))
    field_z = jnp.pad(field_pad, ((0, 0), (1, 1), (0, 0), (0, 0)))
    centre_eta = eta_pad[:, 1 : 1 + row_count, 1 : 1 + col_count]
    diagonal = friction
    summed = jnp.zeros((2, levels, row_count, col_count), jnp.float32)
    for shift_z, shift_x, shift_y, weight in neighbour_offsets():
        linkage = (
            weight
            * 0.5
            * (
                centre_eta
                + eta_z[
                    1 + shift_z : 1 + shift_z + levels,
                    1 + shift_x : 1 + shift_x + row_count,
                    1 + shift_y : 1 + shift_y + col_count,
                ]
            )
        )
        diagonal = diagonal + linkage
        summed = (
            summed
            + linkage[None]
            * field_z[
                :,
                1 + shift_z : 1 + shift_z + levels,
                1 + shift_x : 1 + shift_x + row_count,
                1 + shift_y : 1 + shift_y + col_count,
            ]
        )
    crossed = 0.25 * (
        field_pad[:, :, 2 : 2 + row_count, 2 : 2 + col_count]
        - field_pad[:, :, 2 : 2 + row_count, 0:col_count]
        - field_pad[:, :, 0:row_count, 2 : 2 + col_count]
        + field_pad[:, :, 0:row_count, 0:col_count]
    )
    centre = field_pad[:, :, 1 : 1 + row_count, 1 : 1 + col_count]
    safe_diag = jnp.where(region_mask > 0, diagonal, 1.0)
    result = centre - (summed - cross_gain * centre_eta[None] * crossed[::-1]) / safe_diag
    return result * region_mask


def lower_inverse(factor_low):
    order_n = factor_low.shape[0]
    identity = jnp.eye(order_n, dtype=jnp.float32)
    inverse = jnp.zeros((order_n, order_n), jnp.float32)
    for position in range(order_n):
        earlier = jnp.dot(
            factor_low[position, :position], inverse[:position], precision=lax.Precision.HIGHEST
        )
        inverse = inverse.at[position].set(
            (identity[position] - earlier) / factor_low[position, position]
        )
    return inverse


def cholesky_pass(basis_rows, gram):
    factor_low = jnp.linalg.cholesky(gram)
    return (
        jnp.dot(lower_inverse(factor_low), basis_rows, precision=lax.Precision.HIGHEST),
        factor_low,
    )


def on_device(start_vector, viscosity, friction, shifts):
    levels, row_count, col_count = viscosity.shape
    powers = shifts.shape[0]
    total_count = 2 * levels * row_count * lax.axis_size("gx") * col_count * lax.axis_size("gy")
    krylov = [start_vector]
    coeffs = jnp.stack([viscosity, friction])
    widened = extended(coeffs, (("gx", 2), ("gy", 3)), powers + 1)
    current = extended(start_vector, (("gx", 2), ("gy", 3)), powers)
    row_pos = (
        lax.axis_index("gx") * row_count - (powers + 1) + jnp.arange(row_count + 2 * powers + 2)
    )
    col_pos = (
        lax.axis_index("gy") * col_count - (powers + 1) + jnp.arange(col_count + 2 * powers + 2)
    )
    row_in = (row_pos >= 0) & (row_pos < row_count * lax.axis_size("gx"))
    col_in = (col_pos >= 0) & (col_pos < col_count * lax.axis_size("gy"))
    inside = (row_in[:, None] & col_in[None, :]).astype(jnp.float32)
    for power in range(powers):
        margin = powers - power
        eta_pad = widened[0][
            :,
            power + 1 : power + 1 + row_count + 2 * margin,
            power + 1 : power + 1 + col_count + 2 * margin,
        ]
        fric_part = widened[1][
            :,
            power + 2 : power + row_count + 2 * margin,
            power + 2 : power + col_count + 2 * margin,
        ]
        region = inside[
            power + 2 : power + row_count + 2 * margin, power + 2 : power + col_count + 2 * margin
        ]
        applied = apply_operator(current, eta_pad, fric_part, region)
        current = applied - shifts[power] * current[:, :, 1:-1, 1:-1]
        krylov.append(
            current[:, :, margin - 1 : margin - 1 + row_count, margin - 1 : margin - 1 + col_count]
        )

    def global_gram(basis_rows):
        partial_value = jnp.dot(basis_rows, basis_rows.T, precision=lax.Precision.HIGHEST)
        summed = lax.psum(partial_value, ("gx", "gy"))
        return summed / total_count

    basis_rows = jnp.stack(krylov).reshape(powers + 1, -1)
    ortho_one, low_one = cholesky_pass(basis_rows, global_gram(basis_rows))
    ortho_two, low_two = cholesky_pass(ortho_one, global_gram(ortho_one))
    factor = jnp.dot(low_two.T, low_one.T, precision=lax.Precision.HIGHEST)
    return (ortho_two.reshape(powers + 1, 2, levels, row_count, col_count), factor)


def solution(mesh):
    return jax.shard_map(
        on_device,
        mesh=mesh,
        in_specs=(P(None, None, "gx", "gy"), P(None, "gx", "gy"), P(None, "gx", "gy"), P()),
        out_specs=(P(None, None, None, "gx", "gy"), P()),
        check_vma=False,
    )
```

profile of v0, /device:TPU:0, one launch (start us, length us, event | category | flops | bytes accessed | tf_op | source)
XLA Modules:
  0.0 433.7 jit_solution(16997418263096803367)
XLA Ops:
  1.6 2.4 collective-permute-start
  8.0 5.8 %collective-permute-start.4 = (f32[2,16,9,128]{3,1,2,0:T(8,128)S(1)}, f32[2,16,9,128]{3,1,2,0:T(8,128)S(1)}, u32[]{:S(2)}, u32[]{:S(2)}) collective-permute-start(f32[2,16,9,128]{3,1,2,0:T(8,128)S(1)} %copy.750), channel_id=1, source_target_pairs={{0,8},{8,16},{16,24},{1,9},{9,17},{17,25},{2,10},{10,18},{18,26},{... | collective-permute-start | bytes 442376 | tf_op jit(solution)/shard_map/ppermute | solution.py:16
  23.9 2.0 copy.507
  29.2 5.3 %collective-permute-start.2 = (f32[2,16,32,8]{3,2,1,0:T(8,128)}, f32[2,16,32,8]{3,2,1,0:T(8,128)}, u32[]{:S(2)}, u32[]{:S(2)}) collective-permute-start(f32[2,16,32,8]{3,2,1,0:T(8,128)} %get-tuple-element.459), channel_id=1, source_target_pairs={{0,1},{1,2},{2,3},{3,4},{4,5},{5,6},{6,7},{8,9},{9,10},{10,11},{11... | collective-permute-start | bytes 98312 | tf_op jit(solution)/shard_map/ppermute | solution.py:16
  34.5 2.1 copy.508
  36.6 2.2 copy.506
  38.8 4.0 pad_maximum_fusion
  43.6 1.7 copy.510
  46.6 5.2 %collective-permute-start.6 = (f32[2,16,34,9]{2,1,3,0:T(8,128)}, f32[2,16,34,9]{2,1,3,0:T(8,128)}, u32[]{:S(2)}, u32[]{:S(2)}) collective-permute-start(f32[2,16,34,9]{2,1,3,0:T(8,128)} %get-tuple-element.439), channel_id=1, source_target_pairs={{0,1},{1,2},{2,3},{3,4},{4,5},{5,6},{6,7},{8,9},{9,10},{10,11},{11... | collective-permute-start | bytes 117512 | tf_op jit(solution)/shard_map/ppermute | solution.py:16
  51.8 7.3 %collective-permute-done.2 = f32[2,16,32,8]{3,2,1,0:T(8,128)} collective-permute-done((f32[2,16,32,8]{3,2,1,0:T(8,128)}, f32[2,16,32,8]{3,2,1,0:T(8,128)}, u32[]{:S(2)}, u32[]{:S(2)}) %collective-permute-start.2) | collective-permute-done | bytes 32800 | tf_op jit(solution)/shard_map/ppermute | solution.py:16
  59.1 1.5 pad_maximum_fusion.2
  60.7 1.6 subtract_add_fusion.2
  65.7 3.6 add_select_fusion
  100.1 9.3 %multiply_subtract_fusion.2 = f32[2,16,30,142]{3,2,1,0:T(8,128)S(1)} fusion(f32[2,16,32,144]{3,2,1,0:T(8,128)S(1)} %pad_maximum_fusion.2, f32[2,16,30,142]{3,2,1,0:T(8,128)} %subtract_add_fusion.2, f32[]{:T(128)} %bitcast.5, f32[30,142]{1,0:T(8,128)} %slice.2712, f32[16,30,142]{2,1,0:T(8,128)} %copy.539, f32[16,30,142]{2,1,0:T(8,128)} %copy.538, ...), kind=kLoop, calls=%fused_computation.430 | loop fusion | flops 7906560 | bytes 19227284 | tf_op jit(solution)/shard_map/sub | solution.py:134
  110.3 1.6 subtract_add_fusion.1
  112.8 3.3 add_select_fusion.1
  146.2 9.4 %multiply_subtract_fusion.1 = f32[2,16,28,140]{3,2,1,0:T(8,128)S(1)} fusion(f32[2,16,30,142]{3,2,1,0:T(8,128)S(1)} %multiply_subtract_fusion.2, f32[2,16,28,140]{3,2,1,0:T(8,128)} %subtract_add_fusion.1, f32[]{:T(128)} %bitcast.8, f32[28,140]{1,0:T(8,128)S(1)} %slice.2734, f32[16,28,140]{2,1,0:T(8,128)} %copy.567, f32[16,28,140]{2,1,0:T(8,128)} %copy.566, ...), kind=kLoop, calls=%fused_computation.428 | loop fusion | flops 7275520 | bytes 18546692 | tf_op jit(solution)/shard_map/sub | solution.py:134
  156.4 1.6 subtract_add_fusion
  159.0 3.0 add_select_fusion.2
  191.4 9.2 %multiply_subtract_fusion = f32[2,16,26,138]{3,2,1,0:T(8,128)S(1)} fusion(f32[2,16,28,140]{3,2,1,0:T(8,128)S(1)} %multiply_subtract_fusion.1, f32[2,16,26,138]{3,2,1,0:T(8,128)} %subtract_add_fusion, f32[]{:T(128)} %bitcast.11, f32[26,138]{1,0:T(8,128)S(1)} %slice.2755, f32[16,26,138]{2,1,0:T(8,128)} %copy.595, f32[16,26,138]{2,1,0:T(8,128)} %copy.594, ...), kind=kLoop, calls=%fused_computation.426 | loop fusion | flops 6659328 | bytes 17866756 | tf_op jit(solution)/shard_map/sub | solution.py:134
  201.8 2.7 add_select_fusion.3
  221.8 6.3 %multiply_subtract_fusion.6 = f32[2,16,24,136]{3,2,1,0:T(8,128)S(1)} fusion(f32[2,16,26,138]{3,2,1,0:T(8,128)S(1)} %multiply_subtract_fusion, f32[2,16,24,136]{3,2,1,0:T(8,128)S(1)} %subtract_add_fusion.6, f32[]{:T(128)} %bitcast.14, f32[24,136]{1,0:T(8,128)S(1)} %copy-done.17, f32[16,24,136]{2,1,0:T(8,128)S(1)} %copy.623, f32[16,24,136]{2,1,0:T(8,128)S(1)} %copy.622, ...), kind=kLoop, calls=%fused_computation.710 | loop fusion | flops 6057984 | bytes 18890756 | tf_op jit(solution)/shard_map/sub | solution.py:134
  228.9 2.5 add_select_fusion.4
  237.7 5.0 %multiply_subtract_fusion.5 = f32[2,16,22,134]{3,2,1,0:T(8,128)S(1)} fusion(f32[2,16,24,136]{3,2,1,0:T(8,128)S(1)} %multiply_subtract_fusion.6, f32[2,16,22,134]{3,2,1,0:T(8,128)S(1)} %subtract_add_fusion.5, f32[]{:T(128)} %bitcast.17, f32[22,134]{1,0:T(8,128)S(1)} %copy-done.16, f32[16,22,134]{2,1,0:T(8,128)S(1)} %copy.651, f32[16,22,134]{2,1,0:T(8,128)S(1)} %copy.650, ...), kind=kLoop, calls=%fused_computation.708 | loop fusion | flops 5471488 | bytes 20062724 | tf_op jit(solution)/shard_map/sub | solution.py:134
  243.5 2.3 add_select_fusion.5
  251.5 4.9 %multiply_subtract_fusion.4 = f32[2,16,20,132]{3,2,1,0:T(8,128)S(1)} fusion(f32[2,16,22,134]{3,2,1,0:T(8,128)S(1)} %multiply_subtract_fusion.5, f32[2,16,20,132]{3,2,1,0:T(8,128)S(1)} %subtract_add_fusion.4, f32[]{:T(128)} %bitcast.20, f32[20,132]{1,0:T(8,128)S(1)} %copy-done.15, f32[16,20,132]{2,1,0:T(8,128)S(1)} %copy.679, f32[16,20,132]{2,1,0:T(8,128)S(1)} %copy.678, ...), kind=kLoop, calls=%fused_computation.706 | loop fusion | flops 4899840 | bytes 20023300 | tf_op jit(solution)/shard_map/sub | solution.py:134
  257.3 1.8 add_select_fusion.6
  264.3 4.8 %multiply_subtract_fusion.3 = f32[2,16,18,130]{3,2,1,0:T(8,128)S(1)} fusion(f32[2,16,20,132]{3,2,1,0:T(8,128)S(1)} %multiply_subtract_fusion.4, f32[2,16,18,130]{3,2,1,0:T(8,128)S(1)} %subtract_add_fusion.3, f32[]{:T(128)} %bitcast.23, f32[18,130]{1,0:T(8,128)S(1)} %copy-done.14, f32[16,18,130]{2,1,0:T(8,128)S(1)} %copy.707, f32[16,18,130]{2,1,0:T(8,128)S(1)} %copy.706, ...), kind=kLoop, calls=%fused_computation.704 | loop fusion | flops 4343040 | bytes 19984900 | tf_op jit(solution)/shard_map/sub | solution.py:134
  271.8 1.9 multiply_subtract_fusion.7
  273.8 8.0 %stack.71 = f32[9,2,16,16,128]{4,0,3,2,1:T(8,128)} concatenate(f32[1,2,16,16,128]{4,0,3,2,1:T(1,128)S(1)} %bitcast.330, f32[1,2,16,16,128]{4,0,3,2,1:T(1,128)S(1)} %bitcast.336, f32[1,2,16,16,128]{4,0,3,2,1:T(1,128)S(1)} %bitcast.338, f32[1,2,16,16,128]{4,0,3,2,1:T(1,128)S(1)} %bitcast.340, f32[1,2,16,16,128]{4,0,3,2,1:T(1,128)S(1)} %bitcast.342, ...), dimensions={0} | concatenate | bytes 4718592 | tf_op jit(solution)/shard_map/stack | solution.py:144
  281.8 9.0 %convolution_bitcast_fusion = f32[9,9]{0,1:T(8,128)S(1)} fusion(f32[9,2,16,16,128]{4,0,3,2,1:T(8,128)} %stack.71), kind=kOutput, calls=%fused_computation.146 | convolution fusion | flops 63700992 | bytes 2359620 | tf_op jit(solution)/shard_map/dot_general | solution.py:140
  290.7 40.7 %psum.14 = f32[9,9]{0,1:T(8,128)S(1)} all-reduce(f32[9,9]{0,1:T(8,128)S(1)} %convolution_bitcast_fusion), channel_id=1, replica_groups=mesh['gx'=4,'gy'=8] {'gx','gy'}, use_global_device_ids=true, to_apply=%region_0.1 | all-reduce | flops 81 | bytes 648 | tf_op jit(solution)/shard_map/psum | solution.py:141
  334.4 2.6 subtract_divide_fusion.1
  337.0 1.5 fusion.38
  338.5 1.4 fusion.2
  340.0 1.5 fusion.5
  342.8 1.5 fusion.11
  345.7 1.5 fusion.17
  347.2 8.1 %stack.81 = f32[9,65536]{1,0:T(8,128)} concatenate(f32[1,65536]{1,0:T(1,128)S(1)} %bitcast.331, f32[1,65536]{1,0:T(1,128)S(1)} %bitcast.337, f32[1,65536]{1,0:T(1,128)S(1)} %bitcast.339, f32[1,65536]{1,0:T(1,128)S(1)} %bitcast.341, f32[1,65536]{1,0:T(1,128)S(1)} %bitcast.343, f32[1,65536]{1,0:T(1,128)S(1)} %bitcast.345, f32[1,65536]{1,0:T(1,128)S(1)} %bitcast.347, ...), dimensions={0} | concatenate | bytes 4718592 | tf_op jit(solution)/shard_map/stack | solution.py:144
  355.4 5.4 %fusion.1195 = f32[9,65536]{1,0:T(8,128)S(1)} fusion(f32[9,9]{1,0:T(8,128)S(1)} %scatter.74, f32[9,65536]{1,0:T(8,128)} %stack.81), kind=kOutput, calls=%fused_computation.1486 | convolution fusion | flops 63700992 | bytes 4718916 | tf_op jit(solution)/shard_map/dot_general | solution.py:96
  360.7 1.9 copy-done
  362.7 5.6 %fusion.1196 = f32[9,9]{0,1:T(8,128)S(1)} fusion(f32[9,65536]{1,0:T(8,128)S(1)} %fusion.1195), kind=kOutput, calls=%fused_computation.1487 | convolution fusion | flops 63700992 | bytes 2359620 | tf_op jit(solution)/shard_map/dot_general | solution.py:140
  368.3 40.6 %psum.15 = f32[9,9]{0,1:T(8,128)S(1)} all-reduce(f32[9,9]{0,1:T(8,128)S(1)} %fusion.1196), channel_id=1, replica_groups=mesh['gx'=4,'gy'=8] {'gx','gy'}, use_global_device_ids=true, to_apply=%region_3.5 | all-reduce | flops 81 | bytes 648 | tf_op jit(solution)/shard_map/psum | solution.py:141
  412.7 2.6 subtract_divide_fusion
  416.7 1.5 fusion.20
  424.1 1.5 fusion.35
  425.5 5.4 %fusion.1197 = f32[9,65536]{1,0:T(8,128)S(1)} fusion(f32[9,9]{1,0:T(8,128)S(1)} %scatter.89, f32[9,65536]{1,0:T(8,128)} %copy-done), kind=kOutput, calls=%fused_computation.1488 | convolution fusion | flops 63700992 | bytes 4718916 | tf_op jit(solution)/shard_map/dot_general | solution.py:96
  431.7 1.6 slice.2917
  (391 shorter events, 174.9 us)
Async XLA Ops:
  1.6 25.0 %collective-permute-start = (f32[2,16,8,128]{3,2,1,0:T(8,128)S(1)}, f32[2,16,8,128]{3,2,1,0:T(8,128)S(1)}, u32[]{:S(2)}, u32[]{:S(2)}) collective-permute-start(f32[2,16,8,128]{3,2,1,0:T(8,128)S(1)} %get-tuple-element.464), channel_id=1, source_target_pairs={{0,8},{8,16},{16,24},{1,9},{9,17},{17,25},{2,10},{10,18},{18,26},{... | collective-permute-start | bytes 393224 | tf_op jit(solution)/shard_map/ppermute | solution.py:16
  4.0 22.7 %collective-permute-start.1 = (f32[2,16,8,128]{3,2,1,0:T(8,128)S(1)}, f32[2,16,8,128]{3,2,1,0:T(8,128)S(1)}, u32[]{:S(2)}, u32[]{:S(2)}) collective-permute-start(f32[2,16,8,128]{3,2,1,0:T(8,128)S(1)} %get-tuple-element.463), channel_id=1, source_target_pairs={{8,0},{16,8},{24,16},{9,1},{17,9},{25,17},{10,2},{18,10},{26,18},{... | collective-permute-start | bytes 393224 | tf_op jit(solution)/shard_map/ppermute | solution.py:17
  6.4 19.5 %copy-start.23 = (f32[8]{0:T(128)S(1)}, f32[8]{0:T(128)}, u32[]{:S(2)}) copy-start(f32[8]{0:T(128)} %param.44) | copy-start | bytes 100
  6.4 20.2 %copy-start.1 = (f32[2,16,16,128]{3,2,1,0:T(8,128)S(1)}, f32[2,16,16,128]{3,2,1,0:T(8,128)}, u32[]{:S(2)}) copy-start(f32[2,16,16,128]{3,2,1,0:T(8,128)} %param.41) | copy-start | bytes 786436
  6.5 28.0 %collective-permute-start.5 = (f32[2,16,9,128]{3,1,2,0:T(8,128)S(1)}, f32[2,16,9,128]{3,1,2,0:T(8,128)S(1)}, u32[]{:S(2)}, u32[]{:S(2)}) collective-permute-start(f32[2,16,9,128]{3,1,2,0:T(8,128)S(1)} %copy.751), channel_id=1, source_target_pairs={{8,0},{16,8},{24,16},{9,1},{17,9},{25,17},{10,2},{18,10},{26,18},{... | collective-permute-start | bytes 442376 | tf_op jit(solution)/shard_map/ppermute | solution.py:17
  8.0 28.6 %collective-permute-start.4 = (f32[2,16,9,128]{3,1,2,0:T(8,128)S(1)}, f32[2,16,9,128]{3,1,2,0:T(8,128)S(1)}, u32[]{:S(2)}, u32[]{:S(2)}) collective-permute-start(f32[2,16,9,128]{3,1,2,0:T(8,128)S(1)} %copy.750), channel_id=1, source_target_pairs={{0,8},{8,16},{16,24},{1,9},{9,17},{17,25},{2,10},{10,18},{18,26},{... | collective-permute-start | bytes 442376 | tf_op jit(solution)/shard_map/ppermute | solution.py:16
  27.9 24.0 %collective-permute-start.3 = (f32[2,16,32,8]{3,2,1,0:T(8,128)}, f32[2,16,32,8]{3,2,1,0:T(8,128)S(1)}, u32[]{:S(2)}, u32[]{:S(2)}) collective-permute-start(f32[2,16,32,8]{3,2,1,0:T(8,128)} %get-tuple-element.460), channel_id=1, source_target_pairs={{1,0},{2,1},{3,2},{4,3},{5,4},{6,5},{7,6},{9,8},{10,9},{11,10},{12... | collective-permute-start | bytes 98312 | tf_op jit(solution)/shard_map/ppermute | solution.py:17
  29.2 30.0 %collective-permute-start.2 = (f32[2,16,32,8]{3,2,1,0:T(8,128)}, f32[2,16,32,8]{3,2,1,0:T(8,128)}, u32[]{:S(2)}, u32[]{:S(2)}) collective-permute-start(f32[2,16,32,8]{3,2,1,0:T(8,128)} %get-tuple-element.459), channel_id=1, source_target_pairs={{0,1},{1,2},{2,3},{3,4},{4,5},{5,6},{6,7},{8,9},{9,10},{10,11},{11... | collective-permute-start | bytes 98312 | tf_op jit(solution)/shard_map/ppermute | solution.py:16
  45.3 16.9 %collective-permute-start.7 = (f32[2,16,34,9]{2,1,3,0:T(8,128)}, f32[2,16,34,9]{2,1,3,0:T(8,128)S(1)}, u32[]{:S(2)}, u32[]{:S(2)}) collective-permute-start(f32[2,16,34,9]{2,1,3,0:T(8,128)} %get-tuple-element.440), channel_id=1, source_target_pairs={{1,0},{2,1},{3,2},{4,3},{5,4},{6,5},{7,6},{9,8},{10,9},{11,10},{12... | collective-permute-start | bytes 117512 | tf_op jit(solution)/shard_map/ppermute | solution.py:17
  46.6 16.0 %collective-permute-start.6 = (f32[2,16,34,9]{2,1,3,0:T(8,128)}, f32[2,16,34,9]{2,1,3,0:T(8,128)}, u32[]{:S(2)}, u32[]{:S(2)}) collective-permute-start(f32[2,16,34,9]{2,1,3,0:T(8,128)} %get-tuple-element.439), channel_id=1, source_target_pairs={{0,1},{1,2},{2,3},{3,4},{4,5},{5,6},{6,7},{8,9},{9,10},{10,11},{11... | collective-permute-start | bytes 117512 | tf_op jit(solution)/shard_map/ppermute | solution.py:16
  60.6 3.3 copy-start.4
  64.4 1.3 copy-start.21
  110.3 2.6 copy-start.5
  156.4 2.5 copy-start.6
  200.8 1.0 copy-start.7
  200.8 1.0 copy-start.27
  217.3 4.4 %copy-start.8 = (f32[16,24,136]{2,1,0:T(8,128)S(1)}, f32[16,24,136]{2,1,0:T(8,128)}, u32[]{:S(2)}) copy-start(f32[16,24,136]{2,1,0:T(8,128)} %copy.611) | copy-start | bytes 626692
  217.3 4.4 %copy-start.9 = (f32[16,24,136]{2,1,0:T(8,128)S(1)}, f32[16,24,136]{2,1,0:T(8,128)}, u32[]{:S(2)}) copy-start(f32[16,24,136]{2,1,0:T(8,128)} %copy.610) | copy-start | bytes 626692
  217.3 4.4 %copy-start.10 = (f32[16,24,136]{2,1,0:T(8,128)S(1)}, f32[16,24,136]{2,1,0:T(8,128)}, u32[]{:S(2)}) copy-start(f32[16,24,136]{2,1,0:T(8,128)} %copy.609) | copy-start | bytes 626692
  217.3 4.4 %copy-start.17 = (f32[24,136]{1,0:T(8,128)S(1)}, f32[24,136]{1,0:T(8,128)}, u32[]{:S(2)}) copy-start(f32[24,136]{1,0:T(8,128)} %slice.2776) | copy-start | bytes 39172
  218.3 3.5 copy-start.11
  219.3 2.5 copy-start.12
  220.2 1.5 copy-start.13
  228.2 0.7 copy-start.26
  236.3 1.3 copy-start.16
  242.8 0.7 copy-start.25
  250.0 1.4 copy-start.15
  256.5 0.7 copy-start.24
  263.0 1.3 copy-start.14
  264.3 5.1 %copy-start.28 = (pred[16,128]{1,0:T(8,128)(4,1)S(1)}, pred[16,128]{1,0:T(8,128)(4,1)}, u32[]{:S(2)}) copy-start(pred[16,128]{1,0:T(8,128)(4,1)} %broadcast_compare_fusion.7) | copy-start | bytes 6148
  270.8 1.0 copy-start.22
  271.8 1.9 copy-start.2
  271.8 1.9 copy-start.3
  333.7 3.3 copy-start.18
  360.7 2.0 copy-start
  362.7 49.2 %copy-start.19 = (f32[9,9]{1,0:T(8,128)S(1)}, f32[9,9]{1,0:T(8,128)}, u32[]{:S(2)}) copy-start(f32[9,9]{1,0:T(8,128)} %copy-done.18) | copy-start | bytes 976
  411.2 4.2 copy-start.20
where the time goes:
time: 442 us; the launch traced here: 434 us
  local copies, waits for them, and re-layouts  168 us (38%)
  other arithmetic  104 us (24%)
  blocking collectives  81.3 us (18%)
  matrix products  46.2 us (10%)
  starting transfers between devices  24 us (5%)
  waiting for transfers between devices  7.31 us (2%)
    mul x208, local copies, waits for them, and re-layouts, apply_operator(): weight * 0.5  117 us
    psum x2, blocking collectives, global_gram(): summed = lax.psum(partial_value, ('gx', 'gy'))  81.3 us
    sub x8, other arithmetic, on_device(): current = applied - shifts[power] * current[:, :, 1:-1, 1:-1]  50.8 us
    dot_general x14, matrix products, lower_inverse(): jnp.dot(factor_low[position, :position], inverse[:position], precision=la...  20 us
    select_n x8, other arithmetic, apply_operator(): safe_diag = jnp.where(region_mask > 0, diagonal, 1.0)  20 us
    ppermute x4, starting transfers between devices, extended(): before = lax.ppermute(last, axis, up)  18.7 us
    another operation x2, local copies, waits for them, and re-layouts, on_device(): basis_rows = jnp.stack(krylov).reshape(powers + 1, -1)  16.1 us
    dot_general x2, matrix products, global_gram(): jnp.dot(basis_rows, basis_rows.T, precision=lax.Precision.HIGHEST)  14.6 us
  transfers between devices with their start and end apart: 8, of which 1 were waited for; matrix products, arithmetic and copies ran while one was open for 7% of the time, Pallas kernels for 0%

commit v1 on v0

v1 whole, which is shorter than its diff:
```python
import functools

import jax
import jax.numpy as jnp
from jax import lax
from jax.experimental import pallas as pl
from jax.experimental.pallas import tpu as pltpu
from jax.sharding import PartitionSpec as P

MESH = pl.DeviceIdType.MESH
HALO = 8
GROUP = 2 * HALO
DIRECTIONS = ((1, 0), (-1, 0), (0, 1), (0, -1), (1, 1), (1, -1), (-1, 1), (-1, -1))


def both(lower_ok, upper_ok):
    if lower_ok is None:
        return upper_ok
    if upper_ok is None:
        return lower_ok
    return jnp.logical_and(lower_ok, upper_ok)


def kernel(
    gx_count,
    gy_count,
    start_ref,
    eta_in_ref,
    fric_in_ref,
    shift_ref,
    out_ref,
    factor_ref,
    cur,
    eta,
    fric,
    centre_coef,
    a_mid,
    g_mid,
    a_up,
    g_up,
    a_down,
    g_down,
    packed,
    edge,
    red,
    mine_x,
    mine_y,
    slots_x,
    slots_y,
    splat,
    lower_inv,
    row_send,
    row_recv,
    pack_send,
    pack_recv,
    gx_send,
    gx_recv,
    gy_send,
    gy_recv,
):
    powers = shift_ref.shape[0]
    count = powers + 1
    levels, rows, lanes = eta_in_ref.shape
    wide = rows + 2 * HALO
    me_x, me_y = lax.axis_index("gx"), lax.axis_index("gy")
    total_count = 2.0 * levels * rows * lanes * gx_count * gy_count

    def exists(dx, dy):
        x_ok = {1: me_x < gx_count - 1, -1: me_x > 0, 0: None}[dx]
        y_ok = {1: me_y < gy_count - 1, -1: me_y > 0, 0: None}[dy]
        return both(x_ok, y_ok)

    def device(dx, dy):
        return (jnp.clip(me_x + dx, 0, gx_count - 1), jnp.clip(me_y + dy, 0, gy_count - 1))

    def ring_x(step):
        return (lax.rem(me_x + step, gx_count), me_y)

    def ring_y(step):
        return (me_x, lax.rem(me_y + step, gy_count))

    barrier = pltpu.get_barrier_semaphore()
    for step in range(1, gx_count):
        pl.semaphore_signal(barrier, inc=1, device_id=ring_x(step), device_id_type=MESH)
    for step in range(1, gy_count):
        pl.semaphore_signal(barrier, inc=1, device_id=ring_y(step), device_id_type=MESH)
    for dx, dy in DIRECTIONS[4:]:

        @pl.when(exists(dx, dy))
        def _():
            pl.semaphore_signal(barrier, inc=1, device_id=device(dx, dy), device_id_type=MESH)

    lane = lax.broadcasted_iota(jnp.int32, (wide, lanes), 1)
    row = lax.broadcasted_iota(jnp.int32, (wide, lanes), 0)
    lane_in = lane[:rows]

    def source(field, level):
        if field < 2:
            return start_ref[field, level]
        return (eta_in_ref, fric_in_ref)[field - 2][level]

    for field in range(4):
        for group in range(levels // 8):
            tile = jnp.zeros((rows, lanes), jnp.float32)
            for inner in range(8):
                turned = pltpu.roll(
                    source(field, group * 8 + inner), (GROUP * inner + HALO) % lanes, 1
                )
                tile = jnp.where(lane_in // GROUP == inner, turned, tile)
            packed[field * (levels // 8) + group] = tile

    barrier_x = jnp.where(me_x > 0, 1, 0) + jnp.where(me_x < gx_count - 1, 1, 0)
    barrier_y = jnp.where(me_y > 0, 1, 0) + jnp.where(me_y < gy_count - 1, 1, 0)
    pl.semaphore_wait(barrier, gx_count + gy_count - 2 + barrier_x * barrier_y)

    def row_copies(index):
        dx, dy = DIRECTIONS[index]
        src = pl.ds(rows - HALO, HALO) if dx > 0 else pl.ds(0, HALO)
        dst = pl.ds(0, HALO) if dx > 0 else pl.ds(rows + HALO, HALO)
        inner = pl.ds(1, levels)
        pairs = (
            (start_ref.at[:, :, src], cur.at[0, 0, :, inner, dst]),
            (eta_in_ref.at[:, src], eta.at[0, inner, dst]),
            (fric_in_ref.at[:, src], fric.at[0, :, dst]),
        )
        return [
            pltpu.make_async_remote_copy(
                src_ref=a,
                dst_ref=b,
                send_sem=row_send.at[index, n],
                recv_sem=row_recv.at[index, n],
                device_id=device(dx, dy),
                device_id_type=MESH,
            )
            for n, (a, b) in enumerate(pairs)
        ]

    def pack_copies(index):
        dx, dy = DIRECTIONS[index]
        side = 0 if dy > 0 else 1
        if dx == 0:
            src, dst = pl.ds(0, rows), pl.ds(HALO, rows)
        elif dx > 0:
            src, dst = pl.ds(rows - HALO, HALO), pl.ds(0, HALO)
        else:
            src, dst = pl.ds(0, HALO), pl.ds(rows + HALO, HALO)
        return [
            pltpu.make_async_remote_copy(
                src_ref=packed.at[:, src],
                dst_ref=edge.at[side, :, dst],
                send_sem=pack_send.at[index - 2],
                recv_sem=pack_recv.at[index - 2],
                device_id=device(dx, dy),
                device_id_type=MESH,
            )
        ]

    def copies(index):
        return row_copies(index) if index < 2 else pack_copies(index)

    for index, (dx, dy) in enumerate(DIRECTIONS):

        @pl.when(exists(dx, dy))
        def _():
            for copy in copies(index):
                copy.start()

    zero_tile = jnp.zeros((wide, lanes), jnp.float32)
    for comp in range(2):
        for tile in range(2):
            for slot in range(2):
                cur[slot, tile, comp, 0] = zero_tile
                cur[slot, tile, comp, levels + 1] = zero_tile
        cur[0, 0, comp, 1 : levels + 1, HALO : HALO + rows] = start_ref[comp]
        out_ref[0, comp] = start_ref[comp]
    for tile in range(2):
        eta[tile, 0] = zero_tile
        eta[tile, levels + 1] = zero_tile
    eta[0, 1 : levels + 1, HALO : HALO + rows] = eta_in_ref[...]
    fric[0, :, HALO : HALO + rows] = fric_in_ref[...]
    for index, (dx, dy) in enumerate(DIRECTIONS):
        here = exists(-dx, -dy)

        @pl.when(jnp.logical_not(here))
        def _():
            start = 0 if dx > 0 else (HALO if dx == 0 else rows + HALO)
            size = rows if dx == 0 else HALO
            if dy == 0:
                blank = jnp.zeros((levels, HALO, lanes), jnp.float32)
                for comp in range(2):
                    cur[0, 0, comp, 1 : levels + 1, start : start + size] = blank
                eta[0, 1 : levels + 1, start : start + size] = blank
                fric[0, :, start : start + size] = blank
            else:
                side = 0 if dy > 0 else 1
                edge[side, :, start : start + size] = jnp.zeros(
                    (edge.shape[1], size, lanes), jnp.float32
                )

        @pl.when(here)
        def _():
            for copy in copies(index):
                copy.wait_recv()

    is_edge = (lane < HALO) | (lane >= lanes - HALO)
    for field in range(4):
        for group in range(levels // 8):
            spot = field * (levels // 8) + group
            merged = jnp.where(lane % GROUP >= HALO, edge[1, spot], edge[0, spot])
            for inner in range(8):
                level = group * 8 + inner
                turned = pltpu.roll(merged, (2 * lanes - GROUP * inner - HALO) % lanes, 1)
                turned = jnp.where(is_edge, turned, 0.0)
                if field < 2:
                    cur[0, 1, field, level + 1] = turned
                elif field == 2:
                    eta[1, level + 1] = turned
                else:
                    fric[1, level] = turned

    def from_next(first, second):
        a, b = pltpu.roll(first, lanes - 1, 1), pltpu.roll(second, lanes - 1, 1)
        return jnp.where(lane == lanes - 1, b, a), jnp.where(lane == lanes - 1, a, b)

    def from_last(first, second):
        a, b = pltpu.roll(first, 1, 1), pltpu.roll(second, 1, 1)
        return jnp.where(lane == 0, b, a), jnp.where(lane == 0, a, b)

    def smooth_rows(value):
        pair = value + pltpu.roll(value, wide - 1, 0)
        return pair + pltpu.roll(pair, 1, 0)

    row_ok = ((row >= HALO) | (me_x > 0)) & ((row < HALO + rows) | (me_x < gx_count - 1))
    side_ok = ((lane < HALO) & (me_y < gy_count - 1)) | ((lane >= lanes - HALO) & (me_y > 0))
    inside = (row_ok, row_ok & side_ok)

    def coefficients(level, carry):
        sums = [
            smooth_rows(eta[t, level] + 2.0 * eta[t, level + 1] + eta[t, level + 2])
            for t in range(2)
        ]
        after, before = from_next(*sums), from_last(*sums)
        a_pair, g_pair = [], []
        for t in range(2):
            here = eta[t, level + 1]
            diagonal = (
                fric[t, level] + 6.0 * here + 0.125 * (2.0 * sums[t] + after[t] + before[t])
            )
            inverse = jnp.where(inside[t], 0.125 / jnp.where(inside[t], diagonal, 1.0), 0.0)
            a_pair.append(here * inverse)
            g_pair.append(inverse)
            centre_coef[t, level] = 1.0 + 16.0 * a_pair[t]
            a_mid[t, level] = 2.0 * a_pair[t]
            g_mid[t, level] = 2.0 * g_pair[t]
        for values, up, down in ((a_pair, a_up, a_down), (g_pair, g_up, g_down)):
            ahead, behind = from_last(*values), from_next(*values)
            for t in range(2):
                up[t, level] = ahead[t]
                down[t, level] = behind[t]
        return carry

    lax.fori_loop(0, levels, coefficients, 0)

    def power_step(power, carry):
        slot = lax.rem(power, 2)
        newton = shift_ref[power]

        def level_step(level, inner_carry):
            crossed = [[None, None], [None, None]]
            for t in range(2):
                for comp in range(2):
                    value = cur[slot, t, comp, level + 1]
                    slope = pltpu.roll(value, wide - 1, 0) - pltpu.roll(value, 1, 0)
                    crossed[comp][t] = slope + slope
            for comp in range(2):
                centre, ups, downs = [], [], []
                for t in range(2):
                    below = cur[slot, t, comp, level]
                    value = cur[slot, t, comp, level + 1]
                    above = cur[slot, t, comp, level + 2]
                    plain = smooth_rows(below + 2.0 * value + above)
                    scaled = smooth_rows(
                        eta[t, level] * below
                        + 2.0 * (eta[t, level + 1] * value)
                        + eta[t, level + 2] * above
                    )
                    cross = crossed[1 - comp][t]
                    centre.append(
                        (centre_coef[t, level] - newton) * value
                        - (a_mid[t, level] * plain + g_mid[t, level] * scaled)
                    )
                    ups.append(a_up[t, level] * (plain - cross) + g_up[t, level] * scaled)
                    downs.append(a_down[t, level] * (plain + cross) + g_down[t, level] * scaled)
                after, before = from_next(*ups), from_last(*downs)
                for t in range(2):
                    result = centre[t] - (after[t] + before[t])
                    cur[1 - slot, t, comp, level + 1] = result
                    if t == 0:
                        out_ref[power + 1, comp, level] = result[HALO : HALO + rows]
            return inner_carry

        return lax.fori_loop(0, levels, level_step, carry)

    lax.fori_loop(0, powers, power_step, 0)

    pairs = [(i, j) for i in range(count) for j in range(i + 1)]
    place = {pair: n for n, pair in enumerate(pairs)}
    tiles = (len(pairs) + 7) // 8
    lane_8 = lax.broadcasted_iota(jnp.int32, (8, lanes), 1)

    def add_products(sums, vectors):
        return tuple(total + vectors[i] * vectors[j] for total, (i, j) in zip(sums, pairs))

    zeros = tuple(jnp.zeros((8, lanes), jnp.float32) for _ in pairs)

    def exchange(phase, mine, slots, sends, recvs, me, peers, target):
        copies_out = []
        for step in range(1, peers):
            copy = pltpu.make_async_remote_copy(
                src_ref=mine.at[phase],
                dst_ref=slots.at[phase, me],
                send_sem=sends.at[phase, step],
                recv_sem=recvs.at[phase, step],
                device_id=target(step),
                device_id_type=MESH,
            )
            copy.start()
            copies_out.append(copy)
        slots[phase, me] = mine[phase]
        for copy in copies_out:
            copy.wait()
        total = slots[phase, 0]
        for peer in range(1, peers):
            total = total + slots[phase, peer]
        return total

    def gram_of(sums, phase):
        red[8 * tiles - 8 : 8 * tiles] = jnp.zeros((8, lanes), jnp.float32)
        for n, total in enumerate(sums):
            red[n : n + 1] = jnp.sum(total, axis=0, keepdims=True)
        summed = jnp.sum(red[...], axis=1, keepdims=True)
        tile = jnp.zeros((8, lanes), jnp.float32)
        for t in range(tiles):
            tile = jnp.where(lane_8 == t, summed[8 * t : 8 * t + 8], tile)
        mine_x[phase] = tile
        mine_y[phase] = exchange(
            phase, mine_x, slots_x, gx_send, gx_recv, me_x, gx_count, ring_x
        )
        whole = exchange(phase, mine_y, slots_y, gy_send, gy_recv, me_y, gy_count, ring_y)
        whole = whole / total_count
        for t in range(tiles):
            splat[8 * t : 8 * t + 8] = jnp.broadcast_to(whole[:, t : t + 1], (8, lanes))
        return {pair: splat[n : n + 1] for n, pair in enumerate(pairs)}

    def factorise(gram):
        left = dict(gram)
        low, inv = {}, {}
        for j in range(count):
            root = jnp.sqrt(left[j, j])
            scale = 1.0 / root
            low[j, j], inv[j, j] = root, scale
            for i in range(j + 1, count):
                low[i, j] = left[i, j] * scale
            for i in range(j + 1, count):
                for k in range(j + 1, i + 1):
                    left[i, k] = left[i, k] - low[i, j] * low[k, j]
        for i in range(count):
            for j in range(i):
                total = low[i, j] * inv[j, j]
                for k in range(j + 1, i):
                    total = total + low[i, k] * inv[k, j]
                inv[i, j] = -(total * inv[i, i])
        for pair, n in place.items():
            lower_inv[n : n + 1] = inv[pair]
        return low

    def combine(vectors):
        results = []
        for i in range(count):
            total = lower_inv[place[i, 0] : place[i, 0] + 1] * vectors[0]
            for j in range(1, i + 1):
                total = total + lower_inv[place[i, j] : place[i, j] + 1] * vectors[j]
            results.append(total)
        return results

    def basis_at(spot, half):
        comp, level = spot // levels, lax.rem(spot, levels)
        return [out_ref[n, comp, level, 8 * half : 8 * half + 8] for n in range(count)]

    def gram_step(spot, sums):
        for half in range(rows // 8):
            sums = add_products(sums, basis_at(spot, half))
        return sums

    low_one = factorise(gram_of(lax.fori_loop(0, 2 * levels, gram_step, zeros), 0))

    def ortho_step(spot, sums):
        comp, level = spot // levels, lax.rem(spot, levels)
        for half in range(rows // 8):
            vectors = combine(basis_at(spot, half))
            for n in range(count):
                out_ref[n, comp, level, 8 * half : 8 * half + 8] = vectors[n]
            sums = add_products(sums, vectors)
        return sums

    low_two = factorise(gram_of(lax.fori_loop(0, 2 * levels, ortho_step, zeros), 1))

    def last_step(spot, carry):
        comp, level = spot // levels, lax.rem(spot, levels)
        for half in range(rows // 8):
            vectors = combine(basis_at(spot, half))
            for n in range(count):
                out_ref[n, comp, level, 8 * half : 8 * half + 8] = vectors[n]
        return carry

    lax.fori_loop(0, 2 * levels, last_step, 0)

    fac_row = lax.broadcasted_iota(jnp.int32, (count, count), 0)
    fac_col = lax.broadcasted_iota(jnp.int32, (count, count), 1)
    factor = jnp.zeros((count, count), jnp.float32)
    for i in range(count):
        for j in range(i, count):
            total = low_two[i, i] * low_one[j, i]
            for k in range(i + 1, j + 1):
                total = total + low_two[k, i] * low_one[j, k]
            factor = jnp.where((fac_row == i) & (fac_col == j), total[:, :count], factor)
    factor_ref[...] = factor

    for index, (dx, dy) in enumerate(DIRECTIONS):

        @pl.when(exists(dx, dy))
        def _():
            for copy in copies(index):
                copy.wait_send()


def on_device(gx_count, gy_count, start_vector, viscosity, friction, shifts):
    levels, rows, lanes = viscosity.shape
    count = shifts.shape[0] + 1
    wide = rows + 2 * HALO
    tiles = (count * (count + 1) // 2 + 7) // 8
    f32 = jnp.float32
    coef = pltpu.VMEM((2, levels, wide, lanes), f32)
    dma = pltpu.SemaphoreType.DMA
    vmem = pl.BlockSpec(memory_space=pltpu.VMEM)
    return pl.pallas_call(
        functools.partial(kernel, gx_count, gy_count),
        out_shape=(
            jax.ShapeDtypeStruct((count,) + start_vector.shape, f32),
            jax.ShapeDtypeStruct((count, count), f32),
        ),
        in_specs=[vmem, vmem, vmem, pl.BlockSpec(memory_space=pltpu.SMEM)],
        out_specs=(vmem, vmem),
        scratch_shapes=[
            pltpu.VMEM((2, 2, 2, levels + 2, wide, lanes), f32),
            pltpu.VMEM((2, levels + 2, wide, lanes), f32),
            coef,
            coef,
            coef,
            coef,
            coef,
            coef,
            coef,
            coef,
            pltpu.VMEM((levels // 2, rows, lanes), f32),
            pltpu.VMEM((2, levels // 2, wide, lanes), f32),
            pltpu.VMEM((8 * tiles, lanes), f32),
            pltpu.VMEM((2, 8, lanes), f32),
            pltpu.VMEM((2, 8, lanes), f32),
            pltpu.VMEM((2, gx_count, 8, lanes), f32),
            pltpu.VMEM((2, gy_count, 8, lanes), f32),
            pltpu.VMEM((8 * tiles, lanes), f32),
            pltpu.VMEM((8 * tiles, lanes), f32),
            dma((2, 3)),
            dma((2, 3)),
            dma((6,)),
            dma((6,)),
            dma((2, gx_count)),
            dma((2, gx_count)),
            dma((2, gy_count)),
            dma((2, gy_count)),
        ],
        compiler_params=pltpu.CompilerParams(
            collective_id=0, has_side_effects=True, vmem_limit_bytes=40 * 2**20
        ),
    )(start_vector, viscosity, friction, shifts)


def solution(mesh):
    return jax.shard_map(
        functools.partial(on_device, mesh.shape["gx"], mesh.shape["gy"]),
        mesh=mesh,
        in_specs=(P(None, None, "gx", "gy"), P(None, "gx", "gy"), P(None, "gx", "gy"), P()),
        out_specs=(P(None, None, None, "gx", "gy"), P()),
        check_vma=False,
    )
```

time: 442 us -> 71.5 us (0.16); the launches traced: 434 us -> 71.3 us
  local copies, waits for them, and re-layouts: 168 us -> 5.41 us
  other arithmetic: 104 us -> 0 us
  blocking collectives: 81.3 us -> 0 us
  Pallas kernels: 0 us -> 65.2 us
  matrix products: 46.2 us -> 0 us
  starting transfers between devices: 24 us -> 0 us
  waiting for transfers between devices: 7.31 us -> 0 us
    mul x216 -> x0, local copies, waits for them, and re-layouts: 121 us -> none  [the longest x208 117 us: apply_operator(): weight * 0.5]
    psum x2 -> x0, blocking collectives: 81.3 us -> none  [global_gram(): summed = lax.psum(partial_value, ('gx', 'gy'))]
    pallas_call x0 -> x1, Pallas kernels: none -> 65.2 us  [on_device(): pl.pallas_call(functools.partial(kernel, gx_count, gy_count), out_shape=(...]
    sub x8 -> x0, other arithmetic: 50.8 us -> none  [on_device(): current = applied - shifts[power] * current[:, :, 1:-1, 1:-1]]
    dot_general x19 -> x0, matrix products: 46.2 us -> none  [the longest x14 20 us: lower_inverse(): jnp.dot(factor_low[position, :position], inverse[:position], precision=la...]
    ppermute x8 -> x0, starting transfers between devices: 24 us -> none  [the longest x4 18.7 us: extended(): before = lax.ppermute(last, axis, up)]
    select_n x10 -> x0, other arithmetic: 21.3 us -> none  [the longest x8 20 us: apply_operator(): safe_diag = jnp.where(region_mask > 0, diagonal, 1.0)]
    another operation x3 -> x0, local copies, waits for them, and re-layouts: 18.1 us -> none  [the longest x2 16.1 us: on_device(): basis_rows = jnp.stack(krylov).reshape(powers + 1, -1)]
  transfers between devices with their start and end apart: 8 -> 0, of which waited for: 1 -> 0; matrix products, arithmetic and copies ran while one was open for 7% -> 0% of each run, Pallas kernels for 0% -> 0%
where the time goes in v1:
time: 71.5 us; the launch traced here: 71.3 us
  Pallas kernels  65.2 us (91%)
  local copies, waits for them, and re-layouts  5.41 us (8%)
    pallas_call x1, Pallas kernels, on_device(): pl.pallas_call(functools.partial(kernel, gx_count, gy_count), out_shape=(...  65.2 us
    unnamed x10, local copies, waits for them, and re-layouts  5.41 us

profile of v1, /device:TPU:0, one launch (start us, length us, event | category | flops | bytes accessed | tf_op | source)
XLA Modules:
  0.0 71.3 jit_solution(8543563160775886130)
XLA Ops:
  0.6 0.0 copy-start
  0.6 0.9 %copy-done = f32[2,16,16,128]{3,2,1,0:T(8,128)S(1)} copy-done((f32[2,16,16,128]{3,2,1,0:T(8,128)S(1)}, f32[2,16,16,128]{3,2,1,0:T(8,128)}, u32[]{:S(2)}) %copy-start) | copy-done | bytes 262168
  1.6 0.0 copy-start.1
  1.6 0.9 %copy-done.1 = f32[16,16,128]{2,1,0:T(8,128)S(1)} copy-done((f32[16,16,128]{2,1,0:T(8,128)S(1)}, f32[16,16,128]{2,1,0:T(8,128)}, u32[]{:S(2)}) %copy-start.1) | copy-done | bytes 131096
  2.5 0.0 copy-start.2
  2.5 0.9 %copy-done.2 = f32[16,16,128]{2,1,0:T(8,128)S(1)} copy-done((f32[16,16,128]{2,1,0:T(8,128)S(1)}, f32[16,16,128]{2,1,0:T(8,128)}, u32[]{:S(2)}) %copy-start.2) | copy-done | bytes 131096
  3.4 0.0 copy-start.3
  3.4 0.7 copy-done.3
  4.0 65.2 %shard_map.59 = (f32[9,2,16,16,128]{4,3,2,1,0:T(8,128)S(1)}, f32[9,9]{1,0:T(8,128)S(1)}) custom-call(f32[2,16,16,128]{3,2,1,0:T(8,128)S(1)} %copy-done, f32[16,16,128]{2,1,0:T(8,128)S(1)} %copy-done.1, f32[16,16,128]{2,1,0:T(8,128)S(1)} %copy-done.2, f32[8]{0:T(128)S(1)} %copy-done.3), custom_call_target="tpu_custom_call" | custom-call | tf_op jit(solution)/shard_map/pallas_call | solution.py:446
  69.3 1.4 %copy.8 = f32[9,2,16,16,128]{4,3,2,1,0:T(8,128)} copy(f32[9,2,16,16,128]{4,3,2,1,0:T(8,128)S(1)} %get-tuple-element.4) | data formatting | bytes 4718592
  70.7 0.6 copy.9
Async XLA Ops:
  0.6 1.0 %copy-start = (f32[2,16,16,128]{3,2,1,0:T(8,128)S(1)}, f32[2,16,16,128]{3,2,1,0:T(8,128)}, u32[]{:S(2)}) copy-start(f32[2,16,16,128]{3,2,1,0:T(8,128)} %start_ref.1) | copy-start | bytes 786436
  1.6 0.9 %copy-start.1 = (f32[16,16,128]{2,1,0:T(8,128)S(1)}, f32[16,16,128]{2,1,0:T(8,128)}, u32[]{:S(2)}) copy-start(f32[16,16,128]{2,1,0:T(8,128)} %eta_in_ref.1) | copy-start | bytes 393220
  2.5 0.9 %copy-start.2 = (f32[16,16,128]{2,1,0:T(8,128)S(1)}, f32[16,16,128]{2,1,0:T(8,128)}, u32[]{:S(2)}) copy-start(f32[16,16,128]{2,1,0:T(8,128)} %fric_in_ref.1) | copy-start | bytes 393220
  3.4 0.7 copy-start.3

commit v2 on v1

--- a/solution.py
+++ b/solution.py
@@ -220,11 +220,13 @@
 
     def from_next(first, second):
         a, b = pltpu.roll(first, lanes - 1, 1), pltpu.roll(second, lanes - 1, 1)
-        return jnp.where(lane == lanes - 1, b, a), jnp.where(lane == lanes - 1, a, b)
+        at_end = lane[: first.shape[0]] == lanes - 1
+        return jnp.where(at_end, b, a), jnp.where(at_end, a, b)
 
     def from_last(first, second):
         a, b = pltpu.roll(first, 1, 1), pltpu.roll(second, 1, 1)
-        return jnp.where(lane == 0, b, a), jnp.where(lane == 0, a, b)
+        at_start = lane[: first.shape[0]] == 0
+        return jnp.where(at_start, b, a), jnp.where(at_start, a, b)
 
     def smooth_rows(value):
         pair = value + pltpu.roll(value, wide - 1, 0)
@@ -261,8 +263,10 @@
 
     lax.fori_loop(0, levels, coefficients, 0)
 
-    def power_step(power, carry):
-        slot = lax.rem(power, 2)
+    def power_step(power, carry, final=False):
+        kept = slice(HALO, HALO + rows) if final else slice(0, wide)
+
+        slot = power % 2
         newton = shift_ref[power]
 
         def level_step(level, inner_carry):
@@ -271,37 +275,41 @@
                 for comp in range(2):
                     value = cur[slot, t, comp, level + 1]
                     slope = pltpu.roll(value, wide - 1, 0) - pltpu.roll(value, 1, 0)
-                    crossed[comp][t] = slope + slope
+                    crossed[comp][t] = (slope + slope)[kept]
             for comp in range(2):
                 centre, ups, downs = [], [], []
                 for t in range(2):
                     below = cur[slot, t, comp, level]
                     value = cur[slot, t, comp, level + 1]
                     above = cur[slot, t, comp, level + 2]
-                    plain = smooth_rows(below + 2.0 * value + above)
+                    plain = smooth_rows(below + 2.0 * value + above)[kept]
                     scaled = smooth_rows(
                         eta[t, level] * below
                         + 2.0 * (eta[t, level + 1] * value)
                         + eta[t, level + 2] * above
-                    )
+                    )[kept]
                     cross = crossed[1 - comp][t]
                     centre.append(
-                        (centre_coef[t, level] - newton) * value
-                        - (a_mid[t, level] * plain + g_mid[t, level] * scaled)
+                        (centre_coef[t, level, kept] - newton) * value[kept]
+                        - (a_mid[t, level, kept] * plain + g_mid[t, level, kept] * scaled)
                     )
-                    ups.append(a_up[t, level] * (plain - cross) + g_up[t, level] * scaled)
-                    downs.append(a_down[t, level] * (plain + cross) + g_down[t, level] * scaled)
+                    ups.append(a_up[t, level, kept] * (plain - cross) + g_up[t, level, kept] * scaled)
+                    downs.append(a_down[t, level, kept] * (plain + cross) + g_down[t, level, kept] * scaled)
                 after, before = from_next(*ups), from_last(*downs)
                 for t in range(2):
                     result = centre[t] - (after[t] + before[t])
-                    cur[1 - slot, t, comp, level + 1] = result
-                    if t == 0:
+                    if not final:
+                        cur[1 - slot, t, comp, level + 1] = result
+                    if final and t == 0:
+                        out_ref[power + 1, comp, level] = result
+                    elif t == 0:
                         out_ref[power + 1, comp, level] = result[HALO : HALO + rows]
             return inner_carry
 
         return lax.fori_loop(0, levels, level_step, carry)
 
-    lax.fori_loop(0, powers, power_step, 0)
+    lax.fori_loop(0, powers - 1, power_step, 0)
+    power_step(powers - 1, 0, final=True)
 
     pairs = [(i, j) for i in range(count) for j in range(i + 1)]
     place = {pair: n for n, pair in enumerate(pairs)}

time: 71.5 us -> 69.9 us (0.978)
  Pallas kernels: 65.2 us -> 63.6 us
    pallas_call x1, Pallas kernels: 65.2 us -> 63.6 us  [on_device(): pl.pallas_call(functools.partial(kernel, gx_count, gy_count), out_shape=(...]
where the time goes in v2:
time: 69.9 us; the launch traced here: 69.7 us
  Pallas kernels  63.6 us (91%)
  local copies, waits for them, and re-layouts  5.41 us (8%)
    pallas_call x1, Pallas kernels, on_device(): pl.pallas_call(functools.partial(kernel, gx_count, gy_count), out_shape=(...  63.6 us
    unnamed x10, local copies, waits for them, and re-layouts  5.41 us

profile of v2, /device:TPU:0, one launch (start us, length us, event | category | flops | bytes accessed | tf_op | source)
XLA Modules:
  0.0 69.7 jit_solution(14343621583520645591)
XLA Ops:
  0.6 0.0 copy-start
  0.6 0.9 %copy-done = f32[2,16,16,128]{3,2,1,0:T(8,128)S(1)} copy-done((f32[2,16,16,128]{3,2,1,0:T(8,128)S(1)}, f32[2,16,16,128]{3,2,1,0:T(8,128)}, u32[]{:S(2)}) %copy-start) | copy-done | bytes 262168
  1.6 0.0 copy-start.1
  1.6 0.9 %copy-done.1 = f32[16,16,128]{2,1,0:T(8,128)S(1)} copy-done((f32[16,16,128]{2,1,0:T(8,128)S(1)}, f32[16,16,128]{2,1,0:T(8,128)}, u32[]{:S(2)}) %copy-start.1) | copy-done | bytes 131096
  2.5 0.0 copy-start.2
  2.5 0.9 %copy-done.2 = f32[16,16,128]{2,1,0:T(8,128)S(1)} copy-done((f32[16,16,128]{2,1,0:T(8,128)S(1)}, f32[16,16,128]{2,1,0:T(8,128)}, u32[]{:S(2)}) %copy-start.2) | copy-done | bytes 131096
  3.4 0.0 copy-start.3
  3.4 0.7 copy-done.3
  4.0 63.6 %shard_map.59 = (f32[9,2,16,16,128]{4,3,2,1,0:T(8,128)S(1)}, f32[9,9]{1,0:T(8,128)S(1)}) custom-call(f32[2,16,16,128]{3,2,1,0:T(8,128)S(1)} %copy-done, f32[16,16,128]{2,1,0:T(8,128)S(1)} %copy-done.1, f32[16,16,128]{2,1,0:T(8,128)S(1)} %copy-done.2, f32[8]{0:T(128)S(1)} %copy-done.3), custom_call_target="tpu_custom_call" | custom-call | tf_op jit(solution)/shard_map/pallas_call | solution.py:454
  67.7 1.4 %copy.8 = f32[9,2,16,16,128]{4,3,2,1,0:T(8,128)} copy(f32[9,2,16,16,128]{4,3,2,1,0:T(8,128)S(1)} %get-tuple-element.4) | data formatting | bytes 4718592
  69.1 0.6 copy.9
Async XLA Ops:
  0.6 1.0 %copy-start = (f32[2,16,16,128]{3,2,1,0:T(8,128)S(1)}, f32[2,16,16,128]{3,2,1,0:T(8,128)}, u32[]{:S(2)}) copy-start(f32[2,16,16,128]{3,2,1,0:T(8,128)} %start_ref.1) | copy-start | bytes 786436
  1.6 0.9 %copy-start.1 = (f32[16,16,128]{2,1,0:T(8,128)S(1)}, f32[16,16,128]{2,1,0:T(8,128)}, u32[]{:S(2)}) copy-start(f32[16,16,128]{2,1,0:T(8,128)} %eta_in_ref.1) | copy-start | bytes 393220
  2.5 0.9 %copy-start.2 = (f32[16,16,128]{2,1,0:T(8,128)S(1)}, f32[16,16,128]{2,1,0:T(8,128)}, u32[]{:S(2)}) copy-start(f32[16,16,128]{2,1,0:T(8,128)} %fric_in_ref.1) | copy-start | bytes 393220
  3.4 0.7 copy-start.3

commit v3 on v2

--- a/solution.py
+++ b/solution.py
@@ -30,6 +30,7 @@
     shift_ref,
     out_ref,
     factor_ref,
+    lower_inv,
     cur,
     eta,
     fric,
@@ -48,7 +49,6 @@
     slots_x,
     slots_y,
     splat,
-    lower_inv,
     row_send,
     row_recv,
     pack_send,
@@ -413,16 +413,6 @@
 
     low_two = factorise(gram_of(lax.fori_loop(0, 2 * levels, ortho_step, zeros), 1))
 
-    def last_step(spot, carry):
-        comp, level = spot // levels, lax.rem(spot, levels)
-        for half in range(rows // 8):
-            vectors = combine(basis_at(spot, half))
-            for n in range(count):
-                out_ref[n, comp, level, 8 * half : 8 * half + 8] = vectors[n]
-        return carry
-
-    lax.fori_loop(0, 2 * levels, last_step, 0)
-
     fac_row = lax.broadcasted_iota(jnp.int32, (count, count), 0)
     fac_col = lax.broadcasted_iota(jnp.int32, (count, count), 1)
     factor = jnp.zeros((count, count), jnp.float32)
@@ -442,6 +432,26 @@
                 copy.wait_send()
 
 
+def finish(inverse_ref, basis_ref, out_ref):
+    count, _, depth, rows, _ = out_ref.shape
+    comp, first = pl.program_id(0), pl.program_id(1) * depth
+
+    def one_level(level, carry):
+        for half in range(rows // 8):
+            part = slice(8 * half, 8 * half + 8)
+            vectors = [basis_ref[n, comp, first + level, part] for n in range(count)]
+            spot = 0
+            for i in range(count):
+                total = inverse_ref[spot : spot + 1] * vectors[0]
+                for j in range(1, i + 1):
+                    total = total + inverse_ref[spot + j : spot + j + 1] * vectors[j]
+                out_ref[i, 0, level, part] = total
+                spot += i + 1
+        return carry
+
+    lax.fori_loop(0, depth, one_level, 0)
+
+
 def on_device(gx_count, gy_count, start_vector, viscosity, friction, shifts):
     levels, rows, lanes = viscosity.shape
     count = shifts.shape[0] + 1
@@ -451,14 +461,15 @@
     coef = pltpu.VMEM((2, levels, wide, lanes), f32)
     dma = pltpu.SemaphoreType.DMA
     vmem = pl.BlockSpec(memory_space=pltpu.VMEM)
-    return pl.pallas_call(
+    ortho_one, factor, inverse = pl.pallas_call(
         functools.partial(kernel, gx_count, gy_count),
         out_shape=(
             jax.ShapeDtypeStruct((count,) + start_vector.shape, f32),
             jax.ShapeDtypeStruct((count, count), f32),
+            jax.ShapeDtypeStruct((8 * tiles, lanes), f32),
         ),
         in_specs=[vmem, vmem, vmem, pl.BlockSpec(memory_space=pltpu.SMEM)],
-        out_specs=(vmem, vmem),
+        out_specs=(vmem, vmem, vmem),
         scratch_shapes=[
             pltpu.VMEM((2, 2, 2, levels + 2, wide, lanes), f32),
             pltpu.VMEM((2, levels + 2, wide, lanes), f32),
@@ -477,7 +488,6 @@
             pltpu.VMEM((2, 8, lanes), f32),
             pltpu.VMEM((2, gx_count, 8, lanes), f32),
             pltpu.VMEM((2, gy_count, 8, lanes), f32),
-            pltpu.VMEM((8 * tiles, lanes), f32),
             pltpu.VMEM((8 * tiles, lanes), f32),
             dma((2, 3)),
             dma((2, 3)),
@@ -492,6 +502,17 @@
             collective_id=0, has_side_effects=True, vmem_limit_bytes=40 * 2**20
         ),
     )(start_vector, viscosity, friction, shifts)
+    depth = 8 if levels % 8 == 0 else 1
+    block = pl.BlockSpec((count, 1, depth, rows, lanes), lambda c, z: (0, c, z, 0, 0))
+    orthonormal = pl.pallas_call(
+        finish,
+        grid=(2, levels // depth),
+        out_shape=jax.ShapeDtypeStruct(ortho_one.shape, f32),
+        in_specs=[vmem, vmem],
+        compiler_params=pltpu.CompilerParams(vmem_limit_bytes=12 * 2**20),
+        out_specs=block,
+    )(inverse, ortho_one)
+    return orthonormal, factor
 
 
 def solution(mesh):

time: 69.9 us -> 69.8 us (level)
  local copies, waits for them, and re-layouts: 5.41 us -> 4 us
  Pallas kernels: 63.6 us -> 64.9 us
    pallas_call x0 -> x1, Pallas kernels: none -> 2.46 us  [on_device(): pl.pallas_call(finish, grid=(2, levels // depth), out_shape=jax.ShapeDtyp...]
    unnamed x10 -> x9, local copies, waits for them, and re-layouts: 5.41 us -> 4 us
    pallas_call x1, Pallas kernels: 63.6 us -> 62.5 us  [on_device(): pl.pallas_call(functools.partial(kernel, gx_count, gy_count), out_shape=(...]
where the time goes in v3:
time: 69.8 us; the launch traced here: 69.6 us
  Pallas kernels  64.9 us (93%)
  local copies, waits for them, and re-layouts  4 us (6%)
    pallas_call x1, Pallas kernels, on_device(): pl.pallas_call(functools.partial(kernel, gx_count, gy_count), out_shape=(...  62.5 us
    unnamed x9, local copies, waits for them, and re-layouts  4 us
    pallas_call x1, Pallas kernels, on_device(): pl.pallas_call(finish, grid=(2, levels // depth), out_shape=jax.ShapeDtyp...  2.46 us

profile of v3, /device:TPU:0, one launch (start us, length us, event | category | flops | bytes accessed | tf_op | source)
XLA Modules:
  0.0 69.6 jit_solution(7102850413619591499)
XLA Ops:
  0.6 0.0 copy-start
  0.6 0.9 %copy-done = f32[2,16,16,128]{3,2,1,0:T(8,128)S(1)} copy-done((f32[2,16,16,128]{3,2,1,0:T(8,128)S(1)}, f32[2,16,16,128]{3,2,1,0:T(8,128)}, u32[]{:S(2)}) %copy-start) | copy-done | bytes 262168
  1.6 0.0 copy-start.1
  1.6 0.9 %copy-done.1 = f32[16,16,128]{2,1,0:T(8,128)S(1)} copy-done((f32[16,16,128]{2,1,0:T(8,128)S(1)}, f32[16,16,128]{2,1,0:T(8,128)}, u32[]{:S(2)}) %copy-start.1) | copy-done | bytes 131096
  2.5 0.0 copy-start.2
  2.5 0.9 %copy-done.2 = f32[16,16,128]{2,1,0:T(8,128)S(1)} copy-done((f32[16,16,128]{2,1,0:T(8,128)S(1)}, f32[16,16,128]{2,1,0:T(8,128)}, u32[]{:S(2)}) %copy-start.2) | copy-done | bytes 131096
  3.4 0.0 copy-start.3
  3.4 0.7 copy-done.3
  4.0 62.5 %shard_map.59 = (f32[9,2,16,16,128]{4,3,2,1,0:T(8,128)S(1)}, f32[9,9]{1,0:T(8,128)S(1)}, f32[48,128]{1,0:T(8,128)S(1)}) custom-call(f32[2,16,16,128]{3,2,1,0:T(8,128)S(1)} %copy-done, f32[16,16,128]{2,1,0:T(8,128)S(1)} %copy-done.1, f32[16,16,128]{2,1,0:T(8,128)S(1)} %copy-done.2, f32[8]{0:T(128)S(1)} %copy-done.3), custom_call_target="tpu_custom_call" | custom-call | tf_op jit(solution)/shard_map/pallas_call | solution.py:464
  66.5 2.5 %shard_map.60 = f32[9,2,16,16,128]{4,3,2,1,0:T(8,128)} custom-call(f32[48,128]{1,0:T(8,128)S(1)} %get-tuple-element.5.inverse_ref, f32[9,2,16,16,128]{4,3,2,1,0:T(8,128)S(1)} %get-tuple-element.6.basis_ref), custom_call_target="tpu_custom_call" | custom-call | tf_op jit(solution)/shard_map/pallas_call | solution.py:507
  69.0 0.6 copy.7
Async XLA Ops:
  0.6 1.0 %copy-start = (f32[2,16,16,128]{3,2,1,0:T(8,128)S(1)}, f32[2,16,16,128]{3,2,1,0:T(8,128)}, u32[]{:S(2)}) copy-start(f32[2,16,16,128]{3,2,1,0:T(8,128)} %start_ref.1) | copy-start | bytes 786436
  1.6 0.9 %copy-start.1 = (f32[16,16,128]{2,1,0:T(8,128)S(1)}, f32[16,16,128]{2,1,0:T(8,128)}, u32[]{:S(2)}) copy-start(f32[16,16,128]{2,1,0:T(8,128)} %eta_in_ref.1) | copy-start | bytes 393220
  2.5 0.9 %copy-start.2 = (f32[16,16,128]{2,1,0:T(8,128)S(1)}, f32[16,16,128]{2,1,0:T(8,128)}, u32[]{:S(2)}) copy-start(f32[16,16,128]{2,1,0:T(8,128)} %fric_in_ref.1) | copy-start | bytes 393220
  3.4 0.7 copy-start.3
